TPU v7x, 256 devices: a whole 4x4x8 slice. The times are simulated.
256 devices in a mesh: group: 8 (over x, core), sub: 32 (over y, z).
Axes of the slice: x: 4, y: 4, z: 8, core: 2. Of those that a mesh axis runs over, the one named last changes fastest.
Arguments:
- resid_iface: float32 [256, 16, 4352], P(('group', 'sub')), may hold values from -6 to 6
- resid_inner: float32 [256, 16, 3072], P(('group', 'sub')), may hold values from -6 to 6
- weights: float32 [256, 4352], P(('group', 'sub')), may hold values from 0.25 to 0.75
- nbr: int32 [256, 32], P(('group', 'sub')), may hold values from 0 to 1, as said below
- own2: int32 [256, 128], P(('group', 'sub')), may hold values from 0 to 2047
- cidx: int32 [256, 8], P(('group', 'sub')), may hold values from 0 to 16
- neumann: bfloat16 [256, 17, 256, 256], P(('group', 'sub'))
- dirichlet: bfloat16 [256, 8, 384, 384], P(('group', 'sub'))
- coupling: bfloat16 [256, 8, 256, 384], P(('group', 'sub')), may hold values from -0.375 to 0.375
- coarse_basis: bfloat16 [256, 4352, 128], P(('group', 'sub')), may hold values from -0.5 to 0.5
- group_basis: float32 [16384, 512], P(('group', 'sub')), may hold values from -0.25 to 0.25
- group_inverse: float32 [16384, 2048], P('group', 'sub'), as said below
- top_inverse: float32 [512, 512], replicated, as said below
Outputs:
- interface_out: float32 [256, 16, 4352], P(('group', 'sub'))
- interior_out: float32 [256, 16, 3072], P(('group', 'sub'))
Inputs may be any that keep to these rules, and one draw needn't show every extreme that they name: Symmetric within each group (nbr[(g, q), j] = nbr[(g, j), q]) with nbr[(g, q), q] = 0. `group_inverse`: each matrix of a group is symmetric. `top_inverse`: symmetric.
All inputs are finite; a program needn't handle non-finite values.
Results may differ from a plain program's by a relative error of at most 0.013.
Values may be sent and summed in bfloat16 or wider, within the bound.
A program may use at most 64 MiB of HBM per device.

v0:
```python
import jax
import jax.numpy as jnp
from jax import lax
from jax.sharding import PartitionSpec as P


def padded_2(cells, sides, width):
    for axis, dim in sides:
        count = lax.axis_size(axis)
        ends = count - 1
        head = lax.slice_in_dim(cells, 0, width, axis=dim)
        tail = lax.slice_in_dim(cells, cells.shape[dim] - width, cells.shape[dim], axis=dim)
        cells = jnp.concatenate(
            [
                lax.ppermute(tail, axis, [(i, (i + 1) % count) for i in range(ends)]),
                cells,
                lax.ppermute(head, axis, [((i + 1) % count, i) for i in range(ends)]),
            ],
            axis=dim,
        )
    return cells


def shards(
    resid_iface,
    resid_inner,
    weights,
    nbr,
    own2,
    cidx,
    neumann,
    dirichlet,
    coupling,
    coarse_basis,
    group_basis,
    group_inverse,
    top_inverse,
):
    highest = lax.Precision.HIGHEST
    nsub = lax.axis_size("sub")
    mine = lax.axis_index("sub")
    rows = resid_iface.shape[1]
    width = resid_iface.shape[2]
    slot_width = width // (nsub + 2)
    block_count = neumann.shape[1]
    block_width = neumann.shape[2]
    inner_count = dirichlet.shape[1]
    inner_width = dirichlet.shape[2]
    group_width = group_inverse.shape[0]
    share = group_inverse.shape[1]
    slot_mask = jnp.concatenate([nbr[0].astype(jnp.float32), jnp.ones((2,), jnp.float32)])
    scale = jnp.repeat(slot_mask, slot_width) * weights[0]
    weighted = (scale[None, :] * resid_iface[0]).astype(jnp.bfloat16)
    local0 = jnp.dot(weighted, coarse_basis[0], preferred_element_type=jnp.float32)
    onehot = (own2[0][:, None] == jnp.arange(group_width, dtype=jnp.int32)[None, :]).astype(
        jnp.float32
    )
    contrib = jnp.dot(local0, onehot, precision=highest)
    level2 = lax.psum(contrib.astype(jnp.bfloat16), "sub").astype(jnp.float32)
    level2_mine = lax.dynamic_slice_in_dim(level2, mine * share, share, 1)
    neumann_part = jnp.einsum(
        "rkb,kbc->rkc",
        weighted.reshape(rows, block_count, block_width),
        neumann[0],
        preferred_element_type=jnp.float32,
    ).reshape(rows, width)
    top_term = jnp.dot(level2_mine, group_basis, precision=highest)
    level3 = lax.psum(top_term, ("group", "sub"))
    coarse3 = jnp.dot(level3, top_inverse, precision=highest)
    lifted = lax.dot_general(coarse3, group_basis, (((1,), (1,)), ((), ())), precision=highest)
    coarse2_mine = jnp.dot(level2, group_inverse, precision=highest) + lifted
    coarse2 = lax.all_gather(coarse2_mine.astype(jnp.bfloat16), "sub", axis=1, tiled=True)
    values = jnp.take(coarse2, own2[0], axis=1)
    spread = lax.dot_general(
        values, coarse_basis[0], (((1,), (1,)), ((), ())), preferred_element_type=jnp.float32
    )
    scaled = scale[None, :] * (neumann_part + spread)
    slots = scaled.reshape(rows, nsub + 2, slot_width)
    received = lax.all_to_all(
        slots[:, :nsub, :].astype(jnp.bfloat16), "sub", split_axis=1, concat_axis=1, tiled=True
    ).astype(jnp.float32)
    padded = padded_2(slots[:, nsub:, :], (("group", 1),), 1)
    lower_face = slots[:, nsub, :] + padded[:, 0, :]
    upper_face = slots[:, nsub + 1, :] + padded[:, 3, :]
    total = jnp.concatenate(
        [slots[:, :nsub, :] + received, lower_face[:, None, :], upper_face[:, None, :]], axis=1
    )
    interface_out = total.reshape(rows, width)
    iface_blocks = interface_out.reshape(rows, block_count, block_width).astype(jnp.bfloat16)
    picked = jnp.take(iface_blocks, cidx[0], axis=1)
    pushed = jnp.einsum("rkb,kbc->rkc", picked, coupling[0], preferred_element_type=jnp.float32)
    inner_rhs = (resid_inner[0].reshape(rows, inner_count, inner_width) - pushed).astype(
        jnp.bfloat16
    )
    interior_out = jnp.einsum(
        "rkb,kbc->rkc", inner_rhs, dirichlet[0], preferred_element_type=jnp.float32
    ).reshape(rows, inner_count * inner_width)
    return (interface_out[None], interior_out[None])


def solution(mesh):
    placed = (
        P(("group", "sub"), None, None),
        P(("group", "sub"), None, None),
        P(("group", "sub"), None),
        P(("group", "sub"), None),
        P(("group", "sub"), None),
        P(("group", "sub"), None),
        P(("group", "sub"), None, None, None),
        P(("group", "sub"), None, None, None),
        P(("group", "sub"), None, None, None),
        P(("group", "sub"), None, None),
        P(("group", "sub"), None),
        P("group", "sub"),
        P(),
    )
    return jax.shard_map(
        shards,
        mesh=mesh,
        in_specs=placed,
        out_specs=(P(("group", "sub"), None, None), P(("group", "sub"), None, None)),
        check_vma=False,
    )
```

profile of v0, /device:TPU:1, one launch (start us, length us, event | category | flops | bytes accessed | tf_op | source)
XLA Modules:
  0.0 318.7 jit_solution(4623421728509135453)
XLA Ops:
  7.2 0.0 copy-start
  7.2 0.0 copy-start.2
  7.2 0.0 copy-start.4
  7.2 0.0 copy-start.5
  7.2 0.0 all-reduce.3.cloned.1.call-start
  7.3 0.8 convert_bitcast_fusion
  8.1 0.1 broadcast_bitcast_fusion
  8.1 0.8 fusion.45
  8.9 1.6 fusion.25
  10.5 1.8 convolution_convert_fusion
  12.3 0.0 all-reduce.3.cloned.1.call-update
  12.4 0.0 copy-done.4
  12.4 0.0 copy-done.2
  12.5 0.0 copy-done.5
  12.6 2.0 fusion.7
  14.6 0.7 copy.43
  15.3 0.0 copy-start.1
  15.3 136.0 %all-reduce.3.cloned.1.call-done = bf16[16,2048]{1,0:T(8,128)(2,1)} async-done(((bf16[16,2048]{1,0:T(8,128)(2,1)}), bf16[16,2048]{1,0:T(8,128)(2,1)}) %all-reduce.3.cloned.1.call-update) | async-done | bytes 65552 | tf_op jit(solution)/shard_map/psum | solution.py:59
  151.3 1.7 fusion.47
  153.0 78.0 %psum.15 = f32[16,512]{1,0:T(8,128)S(1)} all-reduce(f32[16,512]{1,0:T(8,128)} %fusion.47), channel_id=1, replica_groups=mesh['group'=8,'sub'=32] {'group','sub'}, use_global_device_ids=true, to_apply=%region_1.0 | all-reduce | flops 8192 | bytes 65536 | tf_op jit(solution)/shard_map/psum | solution.py:68
  231.1 0.0 copy-start.3
  231.1 1.9 fusion.58
  233.0 1.4 fusion.57
  234.4 0.0 copy-done.3
  234.4 0.2 fusion.28
  234.6 35.0 %all-gather = bf16[32,64,16]{1,2,0:T(8,128)(2,1)} all-gather(bf16[1,64,16]{1,2,0:T(8,128)(2,1)S(1)} %fusion.28), channel_id=1, replica_groups=mesh['group'=8,'sub'=32] {'sub'}, dimensions={0}, use_global_device_ids=true | all-gather | bytes 67584 | tf_op jit(solution)/shard_map/all_gather | solution.py:72
  269.6 1.9 copy.41
  271.5 1.8 gather_fusion
  273.3 0.0 copy-done.1
  273.3 2.2 fusion
  275.5 1.0 reshape.101
  276.5 12.7 %collective-permute-start = (f32[16,1,128]{2,1,0:T(1,128)S(1)}, f32[16,1,128]{2,1,0:T(1,128)S(1)}, u32[]{:S(2)}, u32[]{:S(2)}) collective-permute-start(f32[16,1,128]{2,1,0:T(1,128)S(1)} %get-tuple-element.4), channel_id=1, source_target_pairs={{0,32},{32,64},{64,96},{96,128},{128,160},{160,192},{192,224},{1,3... | collective-permute-start | bytes 24584 | tf_op jit(solution)/shard_map/ppermute | solution.py:15
  289.2 1.9 collective-permute-start.1
  291.2 0.7 copy.36
  291.9 5.6 %all-to-all-start = ((bf16[16,32,128]{2,0,1:T(8,128)(2,1)}), bf16[16,32,128]{2,0,1:T(8,128)(2,1)S(1)}, u32[]{:S(2)}, u32[]{:S(2)}) async-start(bf16[16,32,128]{2,0,1:T(8,128)(2,1)} %copy.36), calls=%async_computation | async-start | bytes 262144 | tf_op jit(solution)/shard_map/all_to_all | solution.py:79
  297.5 1.0 copy.45
  298.5 0.0 collective-permute-done
  298.5 0.0 collective-permute-done.1
  298.6 8.8 %all-to-all-done = bf16[16,32,128]{2,0,1:T(8,128)(2,1)S(1)} async-done(((bf16[16,32,128]{2,0,1:T(8,128)(2,1)}), bf16[16,32,128]{2,0,1:T(8,128)(2,1)S(1)}, u32[]{:S(2)}, u32[]{:S(2)}) %all-to-all-start) | async-done | bytes 131104 | tf_op jit(solution)/shard_map/all_to_all | solution.py:79
  307.5 0.1 convert_element_type.48
  307.6 0.6 gather_fusion.1
  308.2 0.0 copy-done
  308.2 2.1 fusion.10
  310.3 0.1 copy.40
  310.4 0.7 broadcast_in_dim_reshape.7
  311.1 0.8 broadcast_in_dim_reshape.6
  (17 shorter events, 0.3 us)
Async XLA Ops:
  7.2 301.0 %copy-start = (bf16[1,8,384,384]{3,2,1,0:T(8,128)(2,1)S(1)}, bf16[1,8,384,384]{3,2,1,0:T(8,128)(2,1)}, u32[]{:S(2)}) copy-start(bf16[1,8,384,384]{3,2,1,0:T(8,128)(2,1)} %param.20) | copy-start | bytes 7077892
  7.2 5.2 %copy-start.2 = (f32[1,16,4352]{2,1,0:T(8,128)S(1)}, f32[1,16,4352]{2,1,0:T(8,128)}, u32[]{:S(2)}) copy-start(f32[1,16,4352]{2,1,0:T(8,128)} %param.13) | copy-start | bytes 835588
  7.2 5.2 %copy-start.4 = (s32[1,128]{1,0:T(1,128)S(1)}, s32[1,128]{1,0:T(1,128)}, u32[]{:S(2)}) copy-start(s32[1,128]{1,0:T(1,128)} %param.17) | copy-start | bytes 1540
  7.2 5.3 %copy-start.5 = (s32[1,8]{1,0:T(1,128)S(1)}, s32[1,8]{1,0:T(1,128)}, u32[]{:S(2)}) copy-start(s32[1,8]{1,0:T(1,128)} %param.18) | copy-start | bytes 100
  7.2 144.1 %all-reduce.3.cloned.1.call-start = ((), (), s32[]{:S(2)}) async-start(), calls=%async_computation.1 | async-start | bytes 131072 | tf_op jit(solution)/shard_map/psum | solution.py:59
  15.3 257.9 %copy-start.1 = (bf16[1,4352,128]{2,1,0:T(8,128)(2,1)S(1)}, bf16[1,4352,128]{2,1,0:T(8,128)(2,1)}, u32[]{:S(2)}) copy-start(bf16[1,4352,128]{2,1,0:T(8,128)(2,1)} %param.22) | copy-start | bytes 3342340
  231.1 3.3 %copy-start.3 = (f32[64,512]{1,0:T(8,128)S(1)}, f32[64,512]{1,0:T(8,128)}, u32[]{:S(2)}) copy-start(f32[64,512]{1,0:T(8,128)} %param.23) | copy-start | bytes 393220
  276.5 22.0 %collective-permute-start = (f32[16,1,128]{2,1,0:T(1,128)S(1)}, f32[16,1,128]{2,1,0:T(1,128)S(1)}, u32[]{:S(2)}, u32[]{:S(2)}) collective-permute-start(f32[16,1,128]{2,1,0:T(1,128)S(1)} %get-tuple-element.4), channel_id=1, source_target_pairs={{0,32},{32,64},{64,96},{96,128},{128,160},{160,192},{192,224},{1,3... | collective-permute-start | bytes 24584 | tf_op jit(solution)/shard_map/ppermute | solution.py:15
  289.2 9.3 %collective-permute-start.1 = (f32[16,1,128]{2,1,0:T(1,128)S(1)}, f32[16,1,128]{2,1,0:T(1,128)S(1)}, u32[]{:S(2)}, u32[]{:S(2)}) collective-permute-start(f32[16,1,128]{2,1,0:T(1,128)S(1)} %get-tuple-element.5), channel_id=1, source_target_pairs={{32,0},{64,32},{96,64},{128,96},{160,128},{192,160},{224,192},{33,... | collective-permute-start | bytes 24584 | tf_op jit(solution)/shard_map/ppermute | solution.py:17
  291.9 15.5 %all-to-all-start = ((bf16[16,32,128]{2,0,1:T(8,128)(2,1)}), bf16[16,32,128]{2,0,1:T(8,128)(2,1)S(1)}, u32[]{:S(2)}, u32[]{:S(2)}) async-start(bf16[16,32,128]{2,0,1:T(8,128)(2,1)} %copy.36), calls=%async_computation | async-start | bytes 262144 | tf_op jit(solution)/shard_map/all_to_all | solution.py:79
Sparse Core Ops, SparseCore 0:
  12.5 138.7 all-reduce.2
where the time goes:
time: 319 us
  waiting for transfers between devices  145 us (45%)
  blocking collectives  113 us (35%)
  starting transfers between devices  20.3 us (6%)
  matrix products  15 us (5%)
  between operations  14.3 us (4%)
  local copies, waits for them, and re-layouts  9.48 us (3%)
    psum x1, waiting for transfers between devices, shards(): level2 = lax.psum(contrib.astype(jnp.bfloat16), 'sub').astype(jnp.float32)  136 us
    psum x1, blocking collectives, shards(): level3 = lax.psum(top_term, ('group', 'sub'))  78 us
    all_gather x1, blocking collectives, shards(): lax.all_gather(coarse2_mine.astype(jnp.bfloat16), 'sub', axis=1, tiled=True)  35 us
    ppermute x1, starting transfers between devices, padded_2(): lax.ppermute(tail, axis, [(i, (i + 1) % count) for i in range(ends)])  12.7 us
    all_to_all x1, waiting for transfers between devices, shards(): lax.all_to_all(slots[:, :nsub, :].astype(jnp.bfloat16), 'sub', split_axis...  8.85 us
  transfers between devices with their start and end apart: 4, of which 2 were waited for; matrix products, arithmetic and copies ran while one was open for 1% of the time, Pallas kernels for 0%

commit v1 on v0

--- a/solution.py
+++ b/solution.py
@@ -65,7 +65,7 @@
         preferred_element_type=jnp.float32,
     ).reshape(rows, width)
     top_term = jnp.dot(level2_mine, group_basis, precision=highest)
-    level3 = lax.psum(top_term, ("group", "sub"))
+    level3 = lax.psum(lax.psum(top_term, "group"), "sub")
     coarse3 = jnp.dot(level3, top_inverse, precision=highest)
     lifted = lax.dot_general(coarse3, group_basis, (((1,), (1,)), ((), ())), precision=highest)
     coarse2_mine = jnp.dot(level2, group_inverse, precision=highest) + lifted

time: 319 us -> 407 us (1.28)
  blocking collectives: 113 us -> 172 us
  starting transfers between devices: 20.3 us -> 49.7 us
    psum x1 -> x2, blocking collectives: 78 us -> 139 us  [shards(): level3 = lax.psum(lax.psum(top_term, 'group'), 'sub')]
    ppermute x1, starting transfers between devices: 12.7 us -> 41 us  [padded_2(): lax.ppermute(tail, axis, [(i, (i + 1) % count) for i in range(ends)])]
where the time goes in v1:
time: 407 us; the launch traced here: 406 us
  blocking collectives  172 us (42%)
  waiting for transfers between devices  145 us (36%)
  starting transfers between devices  49.7 us (12%)
  matrix products  14.4 us (4%)
  between operations  14.3 us (4%)
  local copies, waits for them, and re-layouts  9.48 us (2%)
    psum x2, blocking collectives, shards(): level3 = lax.psum(lax.psum(top_term, 'group'), 'sub')  139 us
    psum x1, waiting for transfers between devices, shards(): level2 = lax.psum(contrib.astype(jnp.bfloat16), 'sub').astype(jnp.float32)  136 us
    ppermute x1, starting transfers between devices, padded_2(): lax.ppermute(tail, axis, [(i, (i + 1) % count) for i in range(ends)])  41 us
    all_gather x1, blocking collectives, shards(): lax.all_gather(coarse2_mine.astype(jnp.bfloat16), 'sub', axis=1, tiled=True)  33.2 us
    all_to_all x1, waiting for transfers between devices, shards(): lax.all_to_all(slots[:, :nsub, :].astype(jnp.bfloat16), 'sub', split_axis...  8.92 us
  transfers between devices with their start and end apart: 4, of which 2 were waited for; matrix products, arithmetic and copies ran while one was open for 1% of the time, Pallas kernels for 0%

profile of v1, /device:TPU:1, one launch (start us, length us, event | category | flops | bytes accessed | tf_op | source)
XLA Modules:
  0.0 406.4 jit_solution(16909981359770521150)
XLA Ops:
  7.2 0.0 copy-start
  7.2 0.0 copy-start.2
  7.2 0.0 copy-start.4
  7.2 0.0 copy-start.5
  7.2 0.0 all-reduce.3.cloned.1.call-start
  7.3 0.8 convert_bitcast_fusion
  8.1 0.1 broadcast_bitcast_fusion
  8.1 0.8 fusion.45
  8.9 1.6 fusion.25
  10.5 1.8 convolution_convert_fusion
  12.3 0.0 all-reduce.3.cloned.1.call-update
  12.4 0.0 copy-done.4
  12.4 0.0 copy-done.2
  12.5 0.0 copy-done.5
  12.6 2.0 fusion.7
  14.6 0.7 copy.43
  15.3 0.0 copy-start.1
  15.3 136.0 %all-reduce.3.cloned.1.call-done = bf16[16,2048]{1,0:T(8,128)(2,1)} async-done(((bf16[16,2048]{1,0:T(8,128)(2,1)}), bf16[16,2048]{1,0:T(8,128)(2,1)}) %all-reduce.3.cloned.1.call-update) | async-done | bytes 65552 | tf_op jit(solution)/shard_map/psum | solution.py:59
  151.3 1.1 fusion.47
  152.4 25.3 %psum.22 = f32[16,512]{1,0:T(8,128)} all-reduce(f32[16,512]{1,0:T(8,128)S(1)} %fusion.47), channel_id=1, replica_groups=mesh['group'=8,'sub'=32] {'group'}, use_global_device_ids=true, to_apply=%region_1.0 | all-reduce | flops 8192 | bytes 65536 | tf_op jit(solution)/shard_map/psum | solution.py:68
  177.8 113.4 %psum.23 = f32[16,512]{1,0:T(8,128)S(1)} all-reduce(f32[16,512]{1,0:T(8,128)} %psum.22), channel_id=1, replica_groups=mesh['group'=8,'sub'=32] {'sub'}, use_global_device_ids=true, to_apply=%region_2.0 | all-reduce | flops 8192 | bytes 65536 | tf_op jit(solution)/shard_map/psum | solution.py:68
  291.1 0.0 copy-start.3
  291.1 1.9 fusion.58
  293.0 1.4 fusion.57
  294.4 0.0 copy-done.3
  294.4 0.2 fusion.28
  294.7 33.2 %all-gather = bf16[32,64,16]{1,2,0:T(8,128)(2,1)} all-gather(bf16[1,64,16]{1,2,0:T(8,128)(2,1)S(1)} %fusion.28), channel_id=1, replica_groups=mesh['group'=8,'sub'=32] {'sub'}, dimensions={0}, use_global_device_ids=true | all-gather | bytes 67584 | tf_op jit(solution)/shard_map/all_gather | solution.py:72
  327.9 1.9 copy.41
  329.8 1.8 gather_fusion
  331.5 0.0 copy-done.1
  331.5 2.2 fusion
  333.7 1.0 reshape.101
  334.8 41.0 %collective-permute-start = (f32[16,1,128]{2,1,0:T(1,128)S(1)}, f32[16,1,128]{2,1,0:T(1,128)S(1)}, u32[]{:S(2)}, u32[]{:S(2)}) collective-permute-start(f32[16,1,128]{2,1,0:T(1,128)S(1)} %get-tuple-element.4), channel_id=1, source_target_pairs={{0,32},{32,64},{64,96},{96,128},{128,160},{160,192},{192,224},{1,3... | collective-permute-start | bytes 24584 | tf_op jit(solution)/shard_map/ppermute | solution.py:15
  375.8 3.1 collective-permute-start.1
  378.9 0.7 copy.36
  379.6 5.5 %all-to-all-start = ((bf16[16,32,128]{2,0,1:T(8,128)(2,1)}), bf16[16,32,128]{2,0,1:T(8,128)(2,1)S(1)}, u32[]{:S(2)}, u32[]{:S(2)}) async-start(bf16[16,32,128]{2,0,1:T(8,128)(2,1)} %copy.36), calls=%async_computation | async-start | bytes 262144 | tf_op jit(solution)/shard_map/all_to_all | solution.py:79
  385.2 1.0 copy.45
  386.2 0.0 collective-permute-done
  386.2 0.0 collective-permute-done.1
  386.2 8.9 %all-to-all-done = bf16[16,32,128]{2,0,1:T(8,128)(2,1)S(1)} async-done(((bf16[16,32,128]{2,0,1:T(8,128)(2,1)}), bf16[16,32,128]{2,0,1:T(8,128)(2,1)S(1)}, u32[]{:S(2)}, u32[]{:S(2)}) %all-to-all-start) | async-done | bytes 131104 | tf_op jit(solution)/shard_map/all_to_all | solution.py:79
  395.3 0.1 convert_element_type.48
  395.4 0.6 gather_fusion.1
  395.9 0.0 copy-done
  395.9 2.1 fusion.10
  398.1 0.1 copy.40
  398.1 0.7 broadcast_in_dim_reshape.7
  398.8 0.8 broadcast_in_dim_reshape.6
  (17 shorter events, 0.3 us)
Async XLA Ops:
  7.2 388.8 %copy-start = (bf16[1,8,384,384]{3,2,1,0:T(8,128)(2,1)S(1)}, bf16[1,8,384,384]{3,2,1,0:T(8,128)(2,1)}, u32[]{:S(2)}) copy-start(bf16[1,8,384,384]{3,2,1,0:T(8,128)(2,1)} %param.20) | copy-start | bytes 7077892
  7.2 5.2 %copy-start.2 = (f32[1,16,4352]{2,1,0:T(8,128)S(1)}, f32[1,16,4352]{2,1,0:T(8,128)}, u32[]{:S(2)}) copy-start(f32[1,16,4352]{2,1,0:T(8,128)} %param.13) | copy-start | bytes 835588
  7.2 5.2 %copy-start.4 = (s32[1,128]{1,0:T(1,128)S(1)}, s32[1,128]{1,0:T(1,128)}, u32[]{:S(2)}) copy-start(s32[1,128]{1,0:T(1,128)} %param.17) | copy-start | bytes 1540
  7.2 5.3 %copy-start.5 = (s32[1,8]{1,0:T(1,128)S(1)}, s32[1,8]{1,0:T(1,128)}, u32[]{:S(2)}) copy-start(s32[1,8]{1,0:T(1,128)} %param.18) | copy-start | bytes 100
  7.2 144.1 %all-reduce.3.cloned.1.call-start = ((), (), s32[]{:S(2)}) async-start(), calls=%async_computation.1 | async-start | bytes 131072 | tf_op jit(solution)/shard_map/psum | solution.py:59
  15.3 316.2 %copy-start.1 = (bf16[1,4352,128]{2,1,0:T(8,128)(2,1)S(1)}, bf16[1,4352,128]{2,1,0:T(8,128)(2,1)}, u32[]{:S(2)}) copy-start(bf16[1,4352,128]{2,1,0:T(8,128)(2,1)} %param.22) | copy-start | bytes 3342340
  291.1 3.3 copy-start.3
  334.8 51.4 %collective-permute-start = (f32[16,1,128]{2,1,0:T(1,128)S(1)}, f32[16,1,128]{2,1,0:T(1,128)S(1)}, u32[]{:S(2)}, u32[]{:S(2)}) collective-permute-start(f32[16,1,128]{2,1,0:T(1,128)S(1)} %get-tuple-element.4), channel_id=1, source_target_pairs={{0,32},{32,64},{64,96},{96,128},{128,160},{160,192},{192,224},{1,3... | collective-permute-start | bytes 24584 | tf_op jit(solution)/shard_map/ppermute | solution.py:15
  375.8 10.4 %collective-permute-start.1 = (f32[16,1,128]{2,1,0:T(1,128)S(1)}, f32[16,1,128]{2,1,0:T(1,128)S(1)}, u32[]{:S(2)}, u32[]{:S(2)}) collective-permute-start(f32[16,1,128]{2,1,0:T(1,128)S(1)} %get-tuple-element.5), channel_id=1, source_target_pairs={{32,0},{64,32},{96,64},{128,96},{160,128},{192,160},{224,192},{33,... | collective-permute-start | bytes 24584 | tf_op jit(solution)/shard_map/ppermute | solution.py:17
  379.6 15.5 %all-to-all-start = ((bf16[16,32,128]{2,0,1:T(8,128)(2,1)}), bf16[16,32,128]{2,0,1:T(8,128)(2,1)S(1)}, u32[]{:S(2)}, u32[]{:S(2)}) async-start(bf16[16,32,128]{2,0,1:T(8,128)(2,1)} %copy.36), calls=%async_computation | async-start | bytes 262144 | tf_op jit(solution)/shard_map/all_to_all | solution.py:79
Sparse Core Ops, SparseCore 0:
  12.5 138.7 all-reduce.2
